TPU v7x, 32 devices: a whole 2x2x4 slice. The times are simulated.
32 devices in a mesh: rep: 2 (over y), mem: 4 (over x, core), tp: 4 (over z).
Axes of the slice: x: 2, y: 2, z: 4, core: 2. Of those that a mesh axis runs over, the one named last changes fastest.
Arguments:
- activations: bfloat16 [4096, 8192], P(('rep', 'mem'), 'tp'), parts along dimension 0, may hold values from -6 to 6
- base_weight: bfloat16 [8192, 1024], P('tp'), may hold values from -0.0625 to 0.0625
- pool_shrink: bfloat16 [128, 64, 8192], P('mem', None, 'tp'), may hold values from -0.0625 to 0.0625
- pool_expand: bfloat16 [128, 65536], P('mem', 'tp'), may hold values from -0.75 to 0.75
- cache_shrink: bfloat16 [32, 64, 8192], P(('rep', 'mem'), None, 'tp'), parts along dimension 0, may hold values from -0.0625 to 0.0625
- cache_expand: bfloat16 [32, 65536], P(('rep', 'mem'), 'tp'), parts along dimension 0, may hold values from -0.75 to 0.75
- adapter_home: int32 [256], P('rep'), parts along dimension 0, may hold values from 0 to 127, as said below
- evict_adapters: int32 [8, 2], P('rep'), parts along dimension 0, may hold values from 0 to 127, as said below
- evict_slots: int32 [8, 2], P(('rep', 'mem')), parts along dimension 0, may hold values from 0 to 3, as said below
- block_slot: int32 [32], P(('rep', 'mem')), parts along dimension 0, may hold values from 0 to 3, as said below
- block_live_rows: int32 [32], P(('rep', 'mem')), parts along dimension 0, may hold values from 32 to 128, as said below
Outputs:
- kv_out: bfloat16 [4096, 1024], P(('rep', 'mem', 'tp')), parts along dimension 0
There are 2 independent parts, one for each index of `rep`. A program takes and returns all parts, laid end to end along the dimension named above; an argument that names none is the same for every part. Nothing has to cross between parts.
Inputs may be any that keep to these rules, and one draw needn't show every extreme that they name: `adapter_home`: a permutation of the pool rows. `evict_adapters`: an adapter a lies on pool device adapter_home[a] // 32; at most 1 of one group's loads lie on one pool device, and every group has exactly 1 on each device that it loads from. `evict_slots`: a group's 2 slots are distinct. `block_slot`: each group's 4 blocks use each of its slots once. `block_live_rows`: some block is full.
All inputs are finite; a program needn't handle non-finite values.
Results may differ from a plain program's by a relative error of at most 0.0029.
Values may be sent and summed in bfloat16 or wider, within the bound.
A program may use at most 64 MiB of HBM per device.

v0:
```python
import jax
import jax.numpy as jnp
from jax import lax
from jax.sharding import PartitionSpec as P

VALUE_FEATURES = 1024
BLOCK = 128
CAP = 1
SLOTS = 4
EVICT = 2


def body(
    activations,
    base_weight,
    pool_shrink,
    pool_expand,
    cache_shrink,
    cache_expand,
    adapter_home,
    evict_adapters,
    evict_slots,
    block_slot,
    block_live_rows,
):
    groups = lax.axis_size("mem")
    tp_count = lax.axis_size("tp")
    group_index = lax.axis_index("mem")
    pool_dev = pool_shrink.shape[0]
    home = adapter_home[evict_adapters]
    owner = home // pool_dev
    position = jnp.arange(EVICT, dtype=jnp.int32)
    same = owner[:, :, None] == owner[:, None, :]
    earlier = position[None, None, :] < position[None, :, None]
    rank = jnp.sum((same & earlier).astype(jnp.int32), axis=2)
    local_row = home - owner * pool_dev
    wanted = (owner == group_index)[:, None, :] & (
        rank[:, None, :] == jnp.arange(CAP, dtype=jnp.int32)[None, :, None]
    )
    send_row = jnp.sum(jnp.where(wanted, local_row[:, None, :], 0), axis=2)
    got_shrink, got_expand = (
        lax.all_to_all(pool_shrink[send_row], "mem", split_axis=0, concat_axis=0, tiled=True),
        lax.all_to_all(pool_expand[send_row], "mem", split_axis=0, concat_axis=0, tiled=True),
    )
    my_owner = lax.dynamic_index_in_dim(owner, group_index, 0, keepdims=False)
    my_rank = lax.dynamic_index_in_dim(rank, group_index, 0, keepdims=False)
    flat = my_owner * CAP + my_rank
    new_shrink = got_shrink.reshape((groups * CAP,) + got_shrink.shape[2:])[flat]
    new_expand = got_expand.reshape(groups * CAP, got_expand.shape[2])[flat]
    targets = evict_slots[0]
    slot_shrink = cache_shrink.at[targets].set(new_shrink)
    slot_expand = cache_expand.at[targets].set(new_expand)
    rows = activations.shape[0]
    nblocks = rows // BLOCK
    blocked = activations.reshape(nblocks, BLOCK, activations.shape[1])
    lowrank_state = jnp.einsum(
        "nbd,nrd->nbr", blocked, slot_shrink[block_slot], preferred_element_type=jnp.float32
    ).reshape(rows, -1)
    row_ids = jnp.arange(rows, dtype=jnp.int32)
    block_hot = (row_ids // BLOCK)[:, None] == jnp.arange(nblocks, dtype=jnp.int32)[None, :]
    row_slot = jnp.sum(jnp.where(block_hot, block_slot[None, :], 0), axis=1)
    row_live = row_ids % BLOCK < jnp.sum(jnp.where(block_hot, block_live_rows[None, :], 0), axis=1)
    slot_hot = row_slot[:, None] == jnp.arange(SLOTS, dtype=jnp.int32)[None, :]
    own = rows // tp_count
    start = lax.axis_index("tp") * own
    zero_value = jnp.zeros((), jnp.bfloat16)
    base_rows = lax.psum_scatter(
        jnp.dot(activations, base_weight, preferred_element_type=jnp.float32),
        "tp",
        scatter_dimension=0,
        tiled=True,
    )
    low_rows = lax.psum_scatter(lowrank_state, "tp", scatter_dimension=0, tiled=True).astype(
        jnp.bfloat16
    )
    full_expand = lax.all_gather(slot_expand, "tp", axis=1, tiled=True).reshape(-1, VALUE_FEATURES)
    own_hot = lax.dynamic_slice_in_dim(slot_hot, start, own, 0)
    chosen = jnp.where(own_hot[:, :, None], low_rows[:, None, :], zero_value).reshape(own, -1)
    total = base_rows + 0.5 * jnp.dot(chosen, full_expand, preferred_element_type=jnp.float32)
    own_live = lax.dynamic_slice_in_dim(row_live, start, own, 0)
    return jnp.where(own_live[:, None], total, 0.0).astype(jnp.bfloat16)


def solution(mesh):
    placed = (
        P(("rep", "mem"), "tp"),
        P("tp", None),
        P("mem", None, "tp"),
        P("mem", "tp"),
        P(("rep", "mem"), None, "tp"),
        P(("rep", "mem"), "tp"),
        P("rep"),
        P("rep", None),
        P(("rep", "mem"), None),
        P(("rep", "mem")),
        P(("rep", "mem")),
    )
    return jax.shard_map(
        body, mesh=mesh, in_specs=placed, out_specs=P(("rep", "mem", "tp"), None), check_vma=False
    )
```

profile of v0, /device:TPU:0, one launch (start us, length us, event | category | flops | bytes accessed | tf_op | source)
XLA Modules:
  0.0 119.9 jit_solution(8353111245675611313)
XLA Ops:
  6.6 0.8 copy-done.5
  7.6 0.6 gather_fusion
  8.6 5.0 %gather_fusion.1 = bf16[4,64,2048]{2,1,0:T(8,128)(2,1)} fusion(bf16[32,64,2048]{2,1,0:T(8,128)(2,1)} %param.13, s32[1024]{0:T(1024)S(1)} %pad_clamp_fusion.2), kind=kCustom, calls=%fused_computation.1 | custom fusion | bytes 2097168 | tf_op jit(solution)/shard_map/gather | solution.py:42
  13.6 4.4 %all-to-all-start = ((bf16[4,1,64,2048]{3,2,1,0:T(8,128)(2,1)}), bf16[4,1,64,2048]{3,2,1,0:T(8,128)(2,1)}, u32[]{:S(2)}, u32[]{:S(2)}) async-start(bf16[4,1,64,2048]{3,2,1,0:T(8,128)(2,1)} %bitcast.35), calls=%async_computation.1 | async-start | bytes 2097152 | tf_op jit(solution)/shard_map/all_to_all | solution.py:42
  18.3 14.8 %all-to-all-done = bf16[4,1,64,2048]{3,2,1,0:T(8,128)(2,1)} async-done(((bf16[4,1,64,2048]{3,2,1,0:T(8,128)(2,1)}), bf16[4,1,64,2048]{3,2,1,0:T(8,128)(2,1)}, u32[]{:S(2)}, u32[]{:S(2)}) %all-to-all-start) | async-done | bytes 1048608 | tf_op jit(solution)/shard_map/all_to_all | solution.py:42
  33.2 2.6 %gather_fusion.2 = bf16[2,64,2048]{2,1,0:T(8,128)(2,1)} fusion(bf16[4,64,2048]{2,1,0:T(8,128)(2,1)} %bitcast.5, s32[1024]{0:T(1024)S(1)} %pad_clamp_fusion.1), kind=kCustom, calls=%fused_computation.2 | custom fusion | bytes 1048584 | tf_op jit(solution)/shard_map/gather | solution.py:48
  35.8 1.7 %scatter_fusion = bf16[4,64,2048]{2,1,0:T(8,128)(2,1)S(1)} fusion(bf16[4,64,2048]{2,1,0:T(8,128)(2,1)S(1)} %copy-done.2, s32[2]{0:T(128)S(1)} %get-tuple-element.7, bf16[2,64,2048]{2,1,0:T(8,128)(2,1)} %gather_fusion.2), kind=kCustom, calls=%fused_computation.6 | custom fusion | bytes 1572872 | tf_op jit(solution)/shard_map/scatter | solution.py:51
  37.4 1.6 %gather_fusion.3 = bf16[4,64,2048]{2,1,0:T(8,128)(2,1)} fusion(bf16[4,64,2048]{2,1,0:T(8,128)(2,1)S(1)} %scatter_fusion, s32[1024]{0:T(1024)S(1)} %pad_clamp_fusion), kind=kCustom, calls=%fused_computation.3 | custom fusion | bytes 2097168 | tf_op jit(solution)/shard_map/gather | solution.py:57
  39.1 2.1 %convolution_bitcast_fusion = f32[4,8,8,128]{3,2,1,0:T(8,128)S(1)} fusion(bf16[4,64,2048]{2,1,0:T(8,128)(2,1)} %gather_fusion.3, bf16[4,128,2048]{2,1,0:T(8,128)(2,1)S(1)} %bitcast.34), kind=kOutput, calls=%fused_computation.12 | convolution fusion | flops 134217728 | bytes 3276800 | tf_op jit(solution)/shard_map/nbd,nrd->nbr/dot_general | solution.py:56
  41.1 0.7 copy.49
  41.9 5.9 %fusion.16 = f32[512,1024]{1,0:T(8,128)} fusion(bf16[512,2048]{1,0:T(8,128)(2,1)S(1)} %copy-done, bf16[2048,1024]{1,0:T(8,128)(2,1)} %param.12), kind=kOutput, calls=%fused_computation.55 | convolution fusion | flops 2147483648 | bytes 8388608 | tf_op jit(solution)/shard_map/dot_general | solution.py:68
  47.8 1.2 copy-done.3
  49.0 0.7 gather_fusion.4
  49.6 0.5 broadcast.263
  50.2 0.8 reduce.3
  50.9 0.8 reshape.256
  51.7 3.3 %all-to-all-start.1 = ((bf16[4,2,8192]{2,1,0:T(2,128)(2,1)}), bf16[4,2,8192]{2,1,0:T(2,128)(2,1)S(1)}, u32[]{:S(2)}, u32[]{:S(2)}) async-start(bf16[4,2,8192]{2,1,0:T(2,128)(2,1)} %reshape.256), calls=%async_computation.3 | async-start | bytes 262144 | tf_op jit(solution)/shard_map/all_to_all | solution.py:43
  55.3 4.3 %all-to-all-done.1 = bf16[4,2,8192]{2,1,0:T(2,128)(2,1)S(1)} async-done(((bf16[4,2,8192]{2,1,0:T(2,128)(2,1)}), bf16[4,2,8192]{2,1,0:T(2,128)(2,1)S(1)}, u32[]{:S(2)}, u32[]{:S(2)}) %all-to-all-start.1) | async-done | bytes 131104 | tf_op jit(solution)/shard_map/all_to_all | solution.py:43
  60.0 1.6 %scatter_custom_fusion.1 = bf16[4,16384]{1,0:T(4,128)(2,1)S(1)} fusion(bf16[4,16384]{1,0:T(4,128)(2,1)S(1)} %copy-done.4, s32[2]{0:T(128)S(1)} %get-tuple-element.7, bf16[4,16384]{1,0:T(4,128)(2,1)S(1)} %bitcast.39, s32[1024]{0:T(1024)S(1)} %pad_clamp_fusion.1), kind=kCustom, calls=%fused_computation.15 | custom fusion | bytes 131072 | tf_op jit(solution)/shard_map/scatter | solution.py:52
  61.6 22.9 %all_gather.3 = bf16[4,65536]{1,0:T(4,128)(2,1)S(1)} all-gather(bf16[4,16384]{1,0:T(4,128)(2,1)S(1)} %scatter_custom_fusion.1), channel_id=1, replica_groups=mesh['rep'=2,'mem'=4,'tp'=4] {'tp'}, dimensions={1}, use_global_device_ids=true | all-gather | bytes 655360 | tf_op jit(solution)/shard_map/all_gather | solution.py:76
  84.5 0.4 reshape.181
  85.0 0.8 convert_element_type.10
  85.7 25.4 %reduce-scatter.3.cloned.1.call-done = f32[128,1024]{1,0:T(8,128)} async-done(((f32[512,1024]{1,0:T(8,128)}), f32[128,1024]{1,0:T(8,128)}) %reduce-scatter.3.cloned.1.call-update) | async-done | bytes 524304 | tf_op jit(solution)/shard_map/reduce_scatter | solution.py:67
  111.1 2.0 %fusion.2 = bf16[128,1024]{1,0:T(8,128)(2,1)} fusion(f32[128,1024]{1,0:T(8,128)} %reduce-scatter.3.cloned.1.call-done, bf16[128,256]{0,1:T(8,128)(2,1)S(1)} %bitcast.38, bf16[256,1024]{1,0:T(8,128)(2,1)S(1)} %reshape.181, pred[128]{0:T(512)(128)(4,1)S(1)} %dynamic_slice.13), kind=kOutput, calls=%fused_computation.11 | convolution fusion | flops 67633152 | bytes 1376384 | tf_op jit(solution)/shard_map/dot_general | solution.py:79
  (47 shorter events, 1.5 us)
Async XLA Ops:
  6.5 32.5 %copy-start = (bf16[512,2048]{1,0:T(8,128)(2,1)S(1)}, bf16[512,2048]{1,0:T(8,128)(2,1)}, u32[]{:S(2)}) copy-start(bf16[512,2048]{1,0:T(8,128)(2,1)} %param.11) | copy-start | bytes 6291460
  6.5 1.0 copy-start.1
  6.5 0.8 copy-start.5
  8.6 9.7 %copy-start.8 = (s32[1,2]{1,0:T(1,128)S(1)}, s32[1,2]{1,0:T(1,128)}, u32[]{:S(2)}) copy-start(s32[1,2]{1,0:T(1,128)} %param.19) | copy-start | bytes 28
  8.6 9.7 %copy-start.6 = (s32[4]{0:T(128)S(1)}, s32[4]{0:T(128)}, u32[]{:S(2)}) copy-start(s32[4]{0:T(128)} %param.20) | copy-start | bytes 52
  13.6 22.1 %copy-start.2 = (bf16[4,64,2048]{2,1,0:T(8,128)(2,1)S(1)}, bf16[4,64,2048]{2,1,0:T(8,128)(2,1)}, u32[]{:S(2)}) copy-start(bf16[4,64,2048]{2,1,0:T(8,128)(2,1)} %param.15) | copy-start | bytes 3145732
  13.6 19.5 %all-to-all-start = ((bf16[4,1,64,2048]{3,2,1,0:T(8,128)(2,1)}), bf16[4,1,64,2048]{3,2,1,0:T(8,128)(2,1)}, u32[]{:S(2)}, u32[]{:S(2)}) async-start(bf16[4,1,64,2048]{3,2,1,0:T(8,128)(2,1)} %bitcast.35), calls=%async_computation.1 | async-start | bytes 2097152 | tf_op jit(solution)/shard_map/all_to_all | solution.py:42
  18.0 67.0 %reduce-scatter.5.cloned.1.call-start = ((), (), s32[]{:S(2)}) async-start(), calls=%async_computation.5 | async-start | bytes 163840 | tf_op jit(solution)/shard_map/reduce_scatter | solution.py:73
  41.8 69.3 %reduce-scatter.3.cloned.1.call-start = ((), (), s32[]{:S(2)}) async-start(), calls=%async_computation.4 | async-start | bytes 2621440 | tf_op jit(solution)/shard_map/reduce_scatter | solution.py:67
  47.7 1.2 %copy-start.3 = (bf16[32,16384]{1,0:T(8,128)(2,1)S(1)}, bf16[32,16384]{1,0:T(8,128)(2,1)}, u32[]{:S(2)}) copy-start(bf16[32,16384]{1,0:T(8,128)(2,1)} %param.14) | copy-start | bytes 3145732
  47.7 7.3 %copy-start.7 = (s32[4]{0:T(128)S(1)}, s32[4]{0:T(128)}, u32[]{:S(2)}) copy-start(s32[4]{0:T(128)} %param.21) | copy-start | bytes 52
  47.7 12.2 %copy-start.4 = (bf16[4,16384]{1,0:T(4,128)(2,1)S(1)}, bf16[4,16384]{1,0:T(4,128)(2,1)}, u32[]{:S(2)}) copy-start(bf16[4,16384]{1,0:T(4,128)(2,1)} %param.16) | copy-start | bytes 393220
  51.7 7.9 %all-to-all-start.1 = ((bf16[4,2,8192]{2,1,0:T(2,128)(2,1)}), bf16[4,2,8192]{2,1,0:T(2,128)(2,1)S(1)}, u32[]{:S(2)}, u32[]{:S(2)}) async-start(bf16[4,2,8192]{2,1,0:T(2,128)(2,1)} %reshape.256), calls=%async_computation.3 | async-start | bytes 262144 | tf_op jit(solution)/shard_map/all_to_all | solution.py:43
Sparse Core Ops, SparseCore 0:
  41.9 20.3 reduce-scatter.4
  64.8 46.2 reduce-scatter.2
where the time goes:
time: 121 us; the launch traced here: 120 us
  waiting for transfers between devices  44.6 us (37%)
  blocking collectives  22.9 us (19%)
  local copies, waits for them, and re-layouts  19.2 us (16%)
  between operations  13.6 us (11%)
  matrix products  9.93 us (8%)
  starting transfers between devices  7.77 us (6%)
  other arithmetic  2.01 us (2%)
    reduce_scatter x1, waiting for transfers between devices, body(): lax.psum_scatter(jnp.dot(activations, base_weight, preferred_element_type...  25.4 us
    all_gather x1, blocking collectives, body(): lax.all_gather(slot_expand, 'tp', axis=1, tiled=True)  22.9 us
    all_to_all x1, waiting for transfers between devices, body(): lax.all_to_all(pool_shrink[send_row], 'mem', split_axis=0, concat_axis=0,...  14.8 us
    dot_general x1, matrix products, body(): jnp.dot(activations, base_weight, preferred_element_type=jnp.float32)  5.87 us
    gather x1, local copies, waits for them, and re-layouts, body(): pool_shrink[send_row]  5.04 us
    all_to_all x1, starting transfers between devices, body(): lax.all_to_all(pool_shrink[send_row], 'mem', split_axis=0, concat_axis=0,...  4.37 us
    all_to_all x1, waiting for transfers between devices, body(): lax.all_to_all(pool_expand[send_row], 'mem', split_axis=0, concat_axis=0,...  4.31 us
    all_to_all x1, starting transfers between devices, body(): lax.all_to_all(pool_expand[send_row], 'mem', split_axis=0, concat_axis=0,...  3.32 us
  transfers between devices with their start and end apart: 4, of which 3 were waited for; matrix products, arithmetic and copies ran while one was open for 10% of the time, Pallas kernels for 0%

commit v1 on v0

--- a/solution.py
+++ b/solution.py
@@ -1,6 +1,10 @@
+import functools
+
 import jax
 import jax.numpy as jnp
 from jax import lax
+from jax.experimental import pallas as pl
+from jax.experimental.pallas import tpu as pltpu
 from jax.sharding import PartitionSpec as P
 
 VALUE_FEATURES = 1024
@@ -10,7 +14,7 @@
 EVICT = 2
 
 
-def body(
+def plain_body(
     activations,
     base_weight,
     pool_shrink,
@@ -81,6 +85,231 @@
     return jnp.where(own_live[:, None], total, 0.0).astype(jnp.bfloat16)
 
 
+CHUNKS = 4
+MESH = pl.DeviceIdType.MESH
+
+
+def kernel(
+    nm, nt, act_h, w_h, psh_h, pex_h, csh_h, cex_h, home, evict, eslot, bslot, live,
+    out,
+    act, w, psh, pst, allsh, alle, ssh, sex, xe, full, pf, own, sb, rb, slow, rlow,
+    loc, pex_sem, s_base, r_base, s_sh, r_sh, s_ex, r_ex, s_xe, r_xe, s_low, r_low,
+):
+    mm = lax.axis_index("mem")
+    mt = lax.axis_index("tp")
+    pool_dev = psh_h.shape[0]
+    ranks = cex_h.shape[1]
+    wide = w_h.shape[1] // CHUNKS
+
+    barrier = pltpu.get_barrier_semaphore()
+    for k in range(1, nt):
+        pl.semaphore_signal(barrier, inc=1, device_id={"tp": lax.rem(mt + k, nt)}, device_id_type=MESH)
+    for k in range(1, nm):
+        pl.semaphore_signal(barrier, inc=1, device_id={"mem": lax.rem(mm + k, nm)}, device_id_type=MESH)
+
+    load_act = pltpu.make_async_copy(act_h, act, loc.at[0])
+    load_act.start()
+    load_w = []
+    for c in range(CHUNKS):
+        load_w.append(pltpu.make_async_copy(w_h.at[:, pl.ds(c * wide, wide)], w.at[c], loc.at[1 + c]))
+        load_w[c].start()
+    load_pex = []
+    for r in range(ranks):
+        load_pex.append(pltpu.make_async_copy(
+            pex_h.at[:, pl.ds(r * VALUE_FEATURES, VALUE_FEATURES)],
+            pst.at[pl.ds(r * pool_dev, pool_dev), :],
+            pex_sem.at[r],
+        ))
+        load_pex[r].start()
+    load_psh = pltpu.make_async_copy(psh_h, psh, loc.at[5])
+    load_psh.start()
+    load_csh = pltpu.make_async_copy(csh_h, allsh.at[pl.ds(0, SLOTS)], loc.at[6])
+    load_csh.start()
+    load_cex = pltpu.make_async_copy(cex_h, alle.at[pl.ds(0, SLOTS)], loc.at[7])
+    load_cex.start()
+
+    def base_copy(c, peer, slot):
+        return pltpu.make_async_remote_copy(
+            src_ref=sb.at[c, peer], dst_ref=rb.at[c, slot],
+            send_sem=s_base.at[c, peer], recv_sem=r_base.at[c, slot],
+            device_id={"tp": peer}, device_id_type=MESH)
+
+    def pair_copy(a, b, ss, rs, axis, peer, slot, base=0):
+        return pltpu.make_async_remote_copy(
+            src_ref=a.at[peer], dst_ref=b.at[base + slot],
+            send_sem=ss.at[peer], recv_sem=rs.at[slot],
+            device_id={axis: peer}, device_id_type=MESH)
+
+    load_act.wait()
+    for c in range(CHUNKS):
+        load_w[c].wait()
+        pf[...] = jnp.dot(act[...], w[c], preferred_element_type=jnp.float32)
+        if c == 0:
+            pl.semaphore_wait(barrier, nt - 1 + nm - 1)
+        for k in range(1, nt):
+            peer = lax.rem(mt + k, nt)
+            sb[c, peer] = pf[pl.ds(pl.multiple_of(peer * BLOCK, BLOCK), BLOCK), :].astype(jnp.bfloat16)
+            base_copy(c, peer, mt).start()
+        own[:, c * wide:(c + 1) * wide] = pf[pl.ds(pl.multiple_of(mt * BLOCK, BLOCK), BLOCK), :]
+
+    def wanted(g):
+        row = jnp.int32(0)
+        for e in range(EVICT):
+            h = home[evict[g, e]]
+            o = lax.div(h, jnp.int32(pool_dev))
+            row = jnp.where(o == mm, h - o * pool_dev, row)
+        return row
+
+    rows = [wanted(g) for g in range(nm)]
+    shape = (nm * ranks, ranks * pool_dev)
+    i = lax.broadcasted_iota(jnp.int32, shape, 0)
+    q = lax.broadcasted_iota(jnp.int32, shape, 1)
+    target = jnp.zeros(shape, jnp.int32)
+    for g in range(nm):
+        target = jnp.where((i >= g * ranks) & (i < (g + 1) * ranks), (i - g * ranks) * pool_dev + rows[g], target)
+    hot = jnp.where(q == target, 1.0, 0.0).astype(jnp.bfloat16)
+    for r in range(ranks):
+        load_pex[r].wait()
+    picked = jnp.dot(hot, pst[...], preferred_element_type=jnp.float32).astype(jnp.bfloat16)
+    sex[...] = picked.reshape(nm, ranks, VALUE_FEATURES)
+    for k in range(1, nm):
+        pair_copy(sex, alle, s_ex, r_ex, "mem", lax.rem(mm + k, nm), mm, SLOTS).start()
+    alle[SLOTS + mm] = sex[mm]
+    load_psh.wait()
+    for k in range(1, nm):
+        g = lax.rem(mm + k, nm)
+        ssh[g] = psh[wanted(g)]
+        pair_copy(ssh, allsh, s_sh, r_sh, "mem", g, mm, SLOTS).start()
+    allsh[SLOTS + mm] = psh[wanted(mm)]
+
+    owner = [lax.div(home[evict[mm, e]], jnp.int32(pool_dev)) for e in range(EVICT)]
+
+    def place(b):
+        c = bslot[b]
+        index = c
+        for e in range(EVICT):
+            index = jnp.where(eslot[0, e] == c, SLOTS + owner[e], index)
+        return index
+
+    load_cex.wait()
+    for k in range(1, nm):
+        pair_copy(sex, alle, s_ex, r_ex, "mem", lax.rem(mm + k, nm), lax.rem(mm + k, nm), SLOTS).wait_recv()
+    for k in range(1, nt):
+        peer = lax.rem(mt + k, nt)
+        xe[peer] = alle[place(peer)]
+        pair_copy(xe, full, s_xe, r_xe, "tp", peer, mt).start()
+    full[mt] = alle[place(mt)]
+
+    load_csh.wait()
+    for k in range(1, nm):
+        pair_copy(ssh, allsh, s_sh, r_sh, "mem", lax.rem(mm + k, nm), lax.rem(mm + k, nm), SLOTS).wait_recv()
+
+    def low_of(b):
+        return lax.dot_general(
+            allsh[place(b)], act[pl.ds(pl.multiple_of(b * BLOCK, BLOCK), BLOCK), :],
+            (((1,), (1,)), ((), ())), preferred_element_type=jnp.float32)
+
+    for k in range(1, nt):
+        peer = lax.rem(mt + k, nt)
+        slow[peer] = low_of(peer)
+        pair_copy(slow, rlow, s_low, r_low, "tp", peer, mt).start()
+    low = low_of(mt)
+    for k in range(1, nt):
+        peer = lax.rem(mt + k, nt)
+        pair_copy(xe, full, s_xe, r_xe, "tp", peer, peer).wait_recv()
+        pair_copy(slow, rlow, s_low, r_low, "tp", peer, peer).wait_recv()
+        low = low + rlow[peer]
+    low = low.T.astype(jnp.bfloat16)
+    here = lax.broadcasted_iota(jnp.int32, (BLOCK, wide), 0) < live[mt]
+    for c in range(CHUNKS):
+        cols = slice(c * wide, (c + 1) * wide)
+        up = full[:, :, cols].reshape(nt * ranks, wide)
+        total = own[:, cols] + 0.5 * jnp.dot(low, up, preferred_element_type=jnp.float32)
+        for k in range(1, nt):
+            peer = lax.rem(mt + k, nt)
+            base_copy(c, peer, peer).wait_recv()
+            total = total + rb[c, peer].astype(jnp.float32)
+        out[:, cols] = jnp.where(here, total, 0.0).astype(jnp.bfloat16)
+
+    for k in range(1, nt):
+        peer = lax.rem(mt + k, nt)
+        for c in range(CHUNKS):
+            base_copy(c, peer, mt).wait_send()
+        pair_copy(xe, full, s_xe, r_xe, "tp", peer, mt).wait_send()
+        pair_copy(slow, rlow, s_low, r_low, "tp", peer, mt).wait_send()
+    for k in range(1, nm):
+        g = lax.rem(mm + k, nm)
+        pair_copy(sex, alle, s_ex, r_ex, "mem", g, mm, SLOTS).wait_send()
+        pair_copy(ssh, allsh, s_sh, r_sh, "mem", g, mm, SLOTS).wait_send()
+
+
+def body(
+    activations,
+    base_weight,
+    pool_shrink,
+    pool_expand,
+    cache_shrink,
+    cache_expand,
+    adapter_home,
+    evict_adapters,
+    evict_slots,
+    block_slot,
+    block_live_rows,
+):
+    nm, nt = lax.axis_size("mem"), lax.axis_size("tp")
+    rows, depth = activations.shape
+    ranks = pool_expand.shape[1] // VALUE_FEATURES
+    if rows != nt * BLOCK or ranks % 16 != 0:
+        return plain_body(
+            activations, base_weight, pool_shrink, pool_expand, cache_shrink, cache_expand,
+            adapter_home, evict_adapters, evict_slots, block_slot, block_live_rows)
+    pool_dev, rank = pool_shrink.shape[:2]
+    wide = VALUE_FEATURES // CHUNKS
+    bf, f32 = jnp.bfloat16, jnp.float32
+    dma = pltpu.SemaphoreType.DMA
+    any_spec = pl.BlockSpec(memory_space=pl.ANY)
+    smem = pl.BlockSpec(memory_space=pltpu.SMEM)
+    return pl.pallas_call(
+        functools.partial(kernel, nm, nt),
+        out_shape=jax.ShapeDtypeStruct((BLOCK, VALUE_FEATURES), bf),
+        in_specs=[any_spec] * 6 + [smem] * 5,
+        out_specs=pl.BlockSpec(memory_space=pltpu.VMEM),
+        scratch_shapes=[
+            pltpu.VMEM((rows, depth), bf),
+            pltpu.VMEM((CHUNKS, depth, wide), bf),
+            pltpu.VMEM((pool_dev, rank, depth), bf),
+            pltpu.VMEM((ranks * pool_dev, VALUE_FEATURES), bf),
+            pltpu.VMEM((SLOTS + nm, rank, depth), bf),
+            pltpu.VMEM((SLOTS + nm, ranks, VALUE_FEATURES), bf),
+            pltpu.VMEM((nm, rank, depth), bf),
+            pltpu.VMEM((nm, ranks, VALUE_FEATURES), bf),
+            pltpu.VMEM((nt, ranks, VALUE_FEATURES), bf),
+            pltpu.VMEM((nt, ranks, VALUE_FEATURES), bf),
+            pltpu.VMEM((rows, wide), f32),
+            pltpu.VMEM((BLOCK, VALUE_FEATURES), f32),
+            pltpu.VMEM((CHUNKS, nt, BLOCK, wide), bf),
+            pltpu.VMEM((CHUNKS, nt, BLOCK, wide), bf),
+            pltpu.VMEM((nt, rank, BLOCK), f32),
+            pltpu.VMEM((nt, rank, BLOCK), f32),
+            dma((8,)),
+            dma((ranks,)),
+            dma((CHUNKS, nt)), dma((CHUNKS, nt)),
+            dma((nm,)), dma((nm,)),
+            dma((nm,)), dma((nm,)),
+            dma((nt,)), dma((nt,)),
+            dma((nt,)), dma((nt,)),
+        ],
+        compiler_params=pltpu.CompilerParams(
+            collective_id=0, has_side_effects=True, vmem_limit_bytes=48 * 1024 * 1024),
+        cost_estimate=pl.CostEstimate(
+            flops=2 * rows * depth * (VALUE_FEATURES + rank), bytes_accessed=16 * 1024 * 1024, transcendentals=0),
+    )(
+        activations, base_weight, pool_shrink, pool_expand, cache_shrink,
+        cache_expand.reshape(SLOTS, ranks, VALUE_FEATURES),
+        adapter_home, evict_adapters, evict_slots, block_slot, block_live_rows,
+    )
+
+
 def solution(mesh):
     placed = (
         P(("rep", "mem"), "tp"),

time: 121 us -> 46.8 us (0.39)
  waiting for transfers between devices: 44.6 us -> 0 us
  Pallas kernels: 0 us -> 37.4 us
  blocking collectives: 22.9 us -> 0 us
  between operations: 13.6 us -> 0.03 us
  local copies, waits for them, and re-layouts: 19.2 us -> 9.07 us
  matrix products: 9.93 us -> 0 us
  starting transfers between devices: 7.77 us -> 0 us
  other arithmetic: 2.01 us -> 0 us
    pallas_call x0 -> x1, Pallas kernels: none -> 37.4 us  [body(): pl.pallas_call(functools.partial(kernel, nm, nt), out_shape=jax.ShapeDtyp...]
    reduce_scatter x2 -> x0, waiting for transfers between devices: 25.4 us -> none  [the longest x1 25.4 us: body(): lax.psum_scatter(jnp.dot(activations, base_weight, preferred_element_type...]
    all_gather x1 -> x0, blocking collectives: 22.9 us -> none  [body(): lax.all_gather(slot_expand, 'tp', axis=1, tiled=True)]
    all_to_all x2 -> x0, waiting for transfers between devices: 19.2 us -> none  [the longest x1 14.8 us: body(): lax.all_to_all(pool_shrink[send_row], 'mem', split_axis=0, concat_axis=0,...]
    gather x8 -> x0, local copies, waits for them, and re-layouts: 11.3 us -> none  [the longest x1 5.04 us: body(): pool_shrink[send_row]]
    dot_general x3 -> x0, matrix products: 9.93 us -> none  [the longest x1 5.87 us: body(): jnp.dot(activations, base_weight, preferred_element_type=jnp.float32)]
    all_to_all x2 -> x0, starting transfers between devices: 7.69 us -> none  [the longest x1 4.37 us: body(): lax.all_to_all(pool_shrink[send_row], 'mem', split_axis=0, concat_axis=0,...]
    unnamed x21 -> x17, local copies, waits for them, and re-layouts: 3.15 us -> 9.07 us
  transfers between devices with their start and end apart: 4 -> 0, of which waited for: 3 -> 0; matrix products, arithmetic and copies ran while one was open for 10% -> 0% of each run, Pallas kernels for 0% -> 0%
where the time goes in v1:
time: 46.8 us; the launch traced here: 46.5 us
  Pallas kernels  37.4 us (80%)
  local copies, waits for them, and re-layouts  9.07 us (19%)
    pallas_call x1, Pallas kernels, body(): pl.pallas_call(functools.partial(kernel, nm, nt), out_shape=jax.ShapeDtyp...  37.4 us
    unnamed x17, local copies, waits for them, and re-layouts  9.07 us

profile of v1, /device:TPU:0, one launch (start us, length us, event | category | flops | bytes accessed | tf_op | source)
XLA Modules:
  0.0 46.5 jit_solution(10042967776190899117)
XLA Ops:
  0.0 0.8 %copy.12.evict = s32[4,2]{1,0:T(4,128)S(1)} copy(s32[4,2]{0,1:T(2,128)} %param.18) | data formatting | bytes 64 | tf_op args[7]
  0.8 0.9 %copy.15 = bf16[1,4,16,1024]{3,2,1,0:T(8,128)(2,1)S(1)} copy(bf16[1,4,16,1024]{3,1,2,0:T(4,128)(2,1)} %bitcast.5) | data formatting | bytes 262144
  1.7 0.0 copy-start
  1.7 1.6 %copy-done = bf16[512,2048]{1,0:T(8,128)(2,1)S(1)} copy-done((bf16[512,2048]{1,0:T(8,128)(2,1)S(1)}, bf16[512,2048]{1,0:T(8,128)(2,1)}, u32[]{:S(2)}) %copy-start) | copy-done | bytes 2097176
  3.3 0.0 copy-start.1
  3.3 1.2 %copy-done.1 = bf16[32,16384]{1,0:T(8,128)(2,1)S(1)} copy-done((bf16[32,16384]{1,0:T(8,128)(2,1)S(1)}, bf16[32,16384]{1,0:T(8,128)(2,1)}, u32[]{:S(2)}) %copy-start.1) | copy-done | bytes 1048600
  4.5 0.0 copy-start.2
  4.5 1.2 %copy-done.2 = bf16[4,64,2048]{2,1,0:T(8,128)(2,1)S(1)} copy-done((bf16[4,64,2048]{2,1,0:T(8,128)(2,1)S(1)}, bf16[4,64,2048]{2,1,0:T(8,128)(2,1)}, u32[]{:S(2)}) %copy-start.2) | copy-done | bytes 1048600
  5.8 0.0 copy-start.3
  5.8 0.7 %copy-done.3 = s32[128]{0:T(128)S(1)} copy-done((s32[128]{0:T(128)S(1)}, s32[128]{0:T(128)}, u32[]{:S(2)}) %copy-start.3) | copy-done | bytes 536
  6.4 0.0 copy-start.4
  6.4 0.7 %copy-done.4 = s32[1,2]{1,0:T(1,128)S(1)} copy-done((s32[1,2]{1,0:T(1,128)S(1)}, s32[1,2]{1,0:T(1,128)}, u32[]{:S(2)}) %copy-start.4) | copy-done | bytes 32
  7.1 0.0 copy-start.5
  7.1 0.7 %copy-done.5 = s32[4]{0:T(128)S(1)} copy-done((s32[4]{0:T(128)S(1)}, s32[4]{0:T(128)}, u32[]{:S(2)}) %copy-start.5) | copy-done | bytes 40
  7.7 0.0 copy-start.6
  7.7 0.7 %copy-done.6 = s32[4]{0:T(128)S(1)} copy-done((s32[4]{0:T(128)S(1)}, s32[4]{0:T(128)}, u32[]{:S(2)}) %copy-start.6) | copy-done | bytes 40
  8.4 37.4 %shard_map.109 = bf16[128,1024]{1,0:T(8,128)(2,1)S(1)} custom-call(bf16[512,2048]{1,0:T(8,128)(2,1)S(1)} %copy-done, bf16[2048,1024]{1,0:T(8,128)(2,1)} %w_h.1, bf16[32,64,2048]{2,1,0:T(8,128)(2,1)} %psh_h.1, bf16[32,16384]{1,0:T(8,128)(2,1)S(1)} %copy-done.1, bf16[4,64,2048]{2,1,0:T(8,128)(2,1)S(1)} %copy-done.2, bf16[4,16,1024]{2,1,0:T(8,128)(2,1)S(1)} %bitcast.4, ...), custom_call_target="tpu_custom_call" | custom-call | flops 2281701376 | bytes 16777216 | tf_op jit(solution)/shard_map/pallas_call | solution.py:272
  45.8 0.7 %copy.17 = bf16[128,1024]{1,0:T(8,128)(2,1)} copy(bf16[128,1024]{1,0:T(8,128)(2,1)S(1)} %shard_map.109) | data formatting | bytes 524288
Async XLA Ops:
  1.7 1.6 %copy-start = (bf16[512,2048]{1,0:T(8,128)(2,1)S(1)}, bf16[512,2048]{1,0:T(8,128)(2,1)}, u32[]{:S(2)}) copy-start(bf16[512,2048]{1,0:T(8,128)(2,1)} %act_h.1) | copy-start | bytes 6291460
  3.3 1.2 %copy-start.1 = (bf16[32,16384]{1,0:T(8,128)(2,1)S(1)}, bf16[32,16384]{1,0:T(8,128)(2,1)}, u32[]{:S(2)}) copy-start(bf16[32,16384]{1,0:T(8,128)(2,1)} %pex_h.1) | copy-start | bytes 3145732
  4.5 1.2 %copy-start.2 = (bf16[4,64,2048]{2,1,0:T(8,128)(2,1)S(1)}, bf16[4,64,2048]{2,1,0:T(8,128)(2,1)}, u32[]{:S(2)}) copy-start(bf16[4,64,2048]{2,1,0:T(8,128)(2,1)} %csh_h.1) | copy-start | bytes 3145732
  5.8 0.7 %copy-start.3 = (s32[128]{0:T(128)S(1)}, s32[128]{0:T(128)}, u32[]{:S(2)}) copy-start(s32[128]{0:T(128)} %home.1) | copy-start | bytes 1540
  6.4 0.7 %copy-start.4 = (s32[1,2]{1,0:T(1,128)S(1)}, s32[1,2]{1,0:T(1,128)}, u32[]{:S(2)}) copy-start(s32[1,2]{1,0:T(1,128)} %eslot.1) | copy-start | bytes 28
  7.1 0.7 %copy-start.5 = (s32[4]{0:T(128)S(1)}, s32[4]{0:T(128)}, u32[]{:S(2)}) copy-start(s32[4]{0:T(128)} %bslot.1) | copy-start | bytes 52
  7.7 0.7 %copy-start.6 = (s32[4]{0:T(128)S(1)}, s32[4]{0:T(128)}, u32[]{:S(2)}) copy-start(s32[4]{0:T(128)} %live.1) | copy-start | bytes 52

commit v2 on v1

--- a/solution.py
+++ b/solution.py
@@ -90,15 +90,21 @@
 
 
 def kernel(
-    nm, nt, act_h, w_h, psh_h, pex_h, csh_h, cex_h, home, evict, eslot, bslot, live,
+    nm, nt, act_h, w_h, psh_h, pex_h, csh_h, cex_h, home_h, evict_h, eslot_h, bslot_h, live_h,
     out,
+    home, evict, eslot, bslot, live, cx, hold, relay,
     act, w, psh, pst, allsh, alle, ssh, sex, xe, full, pf, own, sb, rb, slow, rlow,
-    loc, pex_sem, s_base, r_base, s_sh, r_sh, s_ex, r_ex, s_xe, r_xe, s_low, r_low,
+    loc, int_sem, pex_sem, s_rel, r_rel, s_base, r_base, s_sh, r_sh, s_ex, r_ex, s_xe, r_xe, s_low, r_low,
 ):
     mm = lax.axis_index("mem")
     mt = lax.axis_index("tp")
     pool_dev = psh_h.shape[0]
-    ranks = cex_h.shape[1]
+    ranks = cex_h.shape[1] // VALUE_FEATURES
+    near = mt + 1 - 2 * lax.rem(mt, 2)
+    other = lax.rem(mt + 2, nt)
+    far = nt - 1 - mt
+    edge = (mt == 0) | (mt == nt - 1)
+    inner = (mt > 0) & (mt < nt - 1)
     wide = w_h.shape[1] // CHUNKS
 
     barrier = pltpu.get_barrier_semaphore()
@@ -107,12 +113,17 @@
     for k in range(1, nm):
         pl.semaphore_signal(barrier, inc=1, device_id={"mem": lax.rem(mm + k, nm)}, device_id_type=MESH)
 
+    load_int = []
+    for n, (a, b) in enumerate(((home_h, home), (evict_h, evict), (eslot_h, eslot), (bslot_h, bslot), (live_h, live))):
+        load_int.append(pltpu.make_async_copy(a, b, int_sem.at[n]))
     load_act = pltpu.make_async_copy(act_h, act, loc.at[0])
     load_act.start()
     load_w = []
     for c in range(CHUNKS):
         load_w.append(pltpu.make_async_copy(w_h.at[:, pl.ds(c * wide, wide)], w.at[c], loc.at[1 + c]))
         load_w[c].start()
+    for copy in load_int:
+        copy.start()
     load_pex = []
     for r in range(ranks):
         load_pex.append(pltpu.make_async_copy(
@@ -125,7 +136,7 @@
     load_psh.start()
     load_csh = pltpu.make_async_copy(csh_h, allsh.at[pl.ds(0, SLOTS)], loc.at[6])
     load_csh.start()
-    load_cex = pltpu.make_async_copy(cex_h, alle.at[pl.ds(0, SLOTS)], loc.at[7])
+    load_cex = pltpu.make_async_copy(cex_h, cx, loc.at[7])
     load_cex.start()
 
     def base_copy(c, peer, slot):
@@ -133,6 +144,11 @@
             src_ref=sb.at[c, peer], dst_ref=rb.at[c, slot],
             send_sem=s_base.at[c, peer], recv_sem=r_base.at[c, slot],
             device_id={"tp": peer}, device_id_type=MESH)
+
+    def relay_copy(c):
+        return pltpu.make_async_remote_copy(
+            src_ref=sb.at[c, far], dst_ref=relay.at[c], send_sem=s_rel.at[c], recv_sem=r_rel.at[c],
+            device_id={"tp": near}, device_id_type=MESH)
 
     def pair_copy(a, b, ss, rs, axis, peer, slot, base=0):
         return pltpu.make_async_remote_copy(
@@ -146,16 +162,43 @@
         pf[...] = jnp.dot(act[...], w[c], preferred_element_type=jnp.float32)
         if c == 0:
             pl.semaphore_wait(barrier, nt - 1 + nm - 1)
-        for k in range(1, nt):
-            peer = lax.rem(mt + k, nt)
-            sb[c, peer] = pf[pl.ds(pl.multiple_of(peer * BLOCK, BLOCK), BLOCK), :].astype(jnp.bfloat16)
-            base_copy(c, peer, mt).start()
-        own[:, c * wide:(c + 1) * wide] = pf[pl.ds(pl.multiple_of(mt * BLOCK, BLOCK), BLOCK), :]
+
+        def part(b):
+            return pf[pl.ds(pl.multiple_of(b * BLOCK, BLOCK), BLOCK), :]
+
+        sb[c, far] = part(far).astype(jnp.bfloat16)
+
+        @pl.when(edge)
+        def _():
+            relay_copy(c).start()
+            sb[c, other] = part(other).astype(jnp.bfloat16)
+            base_copy(c, other, mt).start()
+
+        @pl.when(inner)
+        def _():
+            base_copy(c, far, mt).start()
+            hold[c] = part(other)
+
+        sb[c, near] = part(near).astype(jnp.bfloat16)
+
+        @pl.when(inner)
+        def _():
+            base_copy(c, near, mt).start()
+
+        own[:, c * wide:(c + 1) * wide] = part(mt)
+
+    @pl.when(edge)
+    def _():
+        for c in range(CHUNKS):
+            base_copy(c, near, mt).start()
+
+    for copy in load_int:
+        copy.wait()
 
     def wanted(g):
         row = jnp.int32(0)
         for e in range(EVICT):
-            h = home[evict[g, e]]
+            h = home[evict[e, g]]
             o = lax.div(h, jnp.int32(pool_dev))
             row = jnp.where(o == mm, h - o * pool_dev, row)
         return row
@@ -182,7 +225,7 @@
         pair_copy(ssh, allsh, s_sh, r_sh, "mem", g, mm, SLOTS).start()
     allsh[SLOTS + mm] = psh[wanted(mm)]
 
-    owner = [lax.div(home[evict[mm, e]], jnp.int32(pool_dev)) for e in range(EVICT)]
+    owner = [lax.div(home[evict[e, mm]], jnp.int32(pool_dev)) for e in range(EVICT)]
 
     def place(b):
         c = bslot[b]
@@ -191,7 +234,23 @@
             index = jnp.where(eslot[0, e] == c, SLOTS + owner[e], index)
         return index
 
+    @pl.when(inner)
+    def _():
+        for c in range(CHUNKS):
+            relay_copy(c).wait_recv()
+            sb[c, other] = (hold[c] + relay[c].astype(jnp.float32)).astype(jnp.bfloat16)
+            base_copy(c, other, mt).start()
+
     load_cex.wait()
+    shape = (SLOTS * ranks, SLOTS)
+    i = lax.broadcasted_iota(jnp.int32, shape, 0)
+    q = lax.broadcasted_iota(jnp.int32, shape, 1)
+    kept = jnp.zeros((SLOTS * ranks, VALUE_FEATURES), jnp.float32)
+    for r in range(ranks):
+        hot = jnp.where(i == q * ranks + r, 1.0, 0.0).astype(jnp.bfloat16)
+        kept += jnp.dot(
+            hot, cx[:, r * VALUE_FEATURES:(r + 1) * VALUE_FEATURES], preferred_element_type=jnp.float32)
+    alle[0:SLOTS] = kept.astype(jnp.bfloat16).reshape(SLOTS, ranks, VALUE_FEATURES)
     for k in range(1, nm):
         pair_copy(sex, alle, s_ex, r_ex, "mem", lax.rem(mm + k, nm), lax.rem(mm + k, nm), SLOTS).wait_recv()
     for k in range(1, nt):
@@ -221,20 +280,36 @@
         low = low + rlow[peer]
     low = low.T.astype(jnp.bfloat16)
     here = lax.broadcasted_iota(jnp.int32, (BLOCK, wide), 0) < live[mt]
+
+    @pl.when(inner)
+    def _():
+        for c in range(CHUNKS):
+            base_copy(c, far, far).wait_recv()
+            own[:, c * wide:(c + 1) * wide] += rb[c, far].astype(jnp.float32)
+
     for c in range(CHUNKS):
         cols = slice(c * wide, (c + 1) * wide)
         up = full[:, :, cols].reshape(nt * ranks, wide)
         total = own[:, cols] + 0.5 * jnp.dot(low, up, preferred_element_type=jnp.float32)
-        for k in range(1, nt):
-            peer = lax.rem(mt + k, nt)
+        for peer in (near, other):
             base_copy(c, peer, peer).wait_recv()
             total = total + rb[c, peer].astype(jnp.float32)
         out[:, cols] = jnp.where(here, total, 0.0).astype(jnp.bfloat16)
 
+    for c in range(CHUNKS):
+        base_copy(c, near, mt).wait_send()
+        base_copy(c, other, mt).wait_send()
+
+        @pl.when(edge)
+        def _():
+            relay_copy(c).wait_send()
+
+        @pl.when(inner)
+        def _():
+            base_copy(c, far, mt).wait_send()
+
     for k in range(1, nt):
         peer = lax.rem(mt + k, nt)
-        for c in range(CHUNKS):
-            base_copy(c, peer, mt).wait_send()
         pair_copy(xe, full, s_xe, r_xe, "tp", peer, mt).wait_send()
         pair_copy(slow, rlow, s_low, r_low, "tp", peer, mt).wait_send()
     for k in range(1, nm):
@@ -259,7 +334,7 @@
     nm, nt = lax.axis_size("mem"), lax.axis_size("tp")
     rows, depth = activations.shape
     ranks = pool_expand.shape[1] // VALUE_FEATURES
-    if rows != nt * BLOCK or ranks % 16 != 0:
+    if nt != 4 or rows != nt * BLOCK or ranks % 16 != 0:
         return plain_body(
             activations, base_weight, pool_shrink, pool_expand, cache_shrink, cache_expand,
             adapter_home, evict_adapters, evict_slots, block_slot, block_live_rows)
@@ -268,13 +343,20 @@
     bf, f32 = jnp.bfloat16, jnp.float32
     dma = pltpu.SemaphoreType.DMA
     any_spec = pl.BlockSpec(memory_space=pl.ANY)
-    smem = pl.BlockSpec(memory_space=pltpu.SMEM)
     return pl.pallas_call(
         functools.partial(kernel, nm, nt),
         out_shape=jax.ShapeDtypeStruct((BLOCK, VALUE_FEATURES), bf),
-        in_specs=[any_spec] * 6 + [smem] * 5,
+        in_specs=[any_spec] * 11,
         out_specs=pl.BlockSpec(memory_space=pltpu.VMEM),
         scratch_shapes=[
+            pltpu.SMEM(adapter_home.shape, jnp.int32),
+            pltpu.SMEM(evict_adapters.shape[::-1], jnp.int32),
+            pltpu.SMEM(evict_slots.shape, jnp.int32),
+            pltpu.SMEM(block_slot.shape, jnp.int32),
+            pltpu.SMEM(block_live_rows.shape, jnp.int32),
+            pltpu.VMEM(cache_expand.shape, bf),
+            pltpu.VMEM((CHUNKS, BLOCK, wide), f32),
+            pltpu.VMEM((CHUNKS, BLOCK, wide), bf),
             pltpu.VMEM((rows, depth), bf),
             pltpu.VMEM((CHUNKS, depth, wide), bf),
             pltpu.VMEM((pool_dev, rank, depth), bf),
@@ -292,7 +374,9 @@
             pltpu.VMEM((nt, rank, BLOCK), f32),
             pltpu.VMEM((nt, rank, BLOCK), f32),
             dma((8,)),
+            dma((5,)),
             dma((ranks,)),
+            dma((CHUNKS,)), dma((CHUNKS,)),
             dma((CHUNKS, nt)), dma((CHUNKS, nt)),
             dma((nm,)), dma((nm,)),
             dma((nm,)), dma((nm,)),
@@ -300,13 +384,13 @@
             dma((nt,)), dma((nt,)),
         ],
         compiler_params=pltpu.CompilerParams(
-            collective_id=0, has_side_effects=True, vmem_limit_bytes=48 * 1024 * 1024),
+            collective_id=0, has_side_effects=True, vmem_limit_bytes=60 * 1024 * 1024),
         cost_estimate=pl.CostEstimate(
             flops=2 * rows * depth * (VALUE_FEATURES + rank), bytes_accessed=16 * 1024 * 1024, transcendentals=0),
     )(
         activations, base_weight, pool_shrink, pool_expand, cache_shrink,
-        cache_expand.reshape(SLOTS, ranks, VALUE_FEATURES),
-        adapter_home, evict_adapters, evict_slots, block_slot, block_live_rows,
+        cache_expand,
+        adapter_home, evict_adapters.T, evict_slots, block_slot, block_live_rows,
     )
 
 

time: 46.8 us -> 34.2 us (0.73)
  local copies, waits for them, and re-layouts: 9.07 us -> 1.67 us
  Pallas kernels: 37.4 us -> 32.4 us
    unnamed x17 -> x1, local copies, waits for them, and re-layouts: 9.07 us -> 1.67 us
    pallas_call x1, Pallas kernels: 37.4 us -> 32.4 us  [body(): pl.pallas_call(functools.partial(kernel, nm, nt), out_shape=jax.ShapeDtyp...]
where the time goes in v2:
time: 34.2 us; the launch traced here: 34.1 us
  Pallas kernels  32.4 us (95%)
  local copies, waits for them, and re-layouts  1.67 us (5%)
    pallas_call x1, Pallas kernels, body(): pl.pallas_call(functools.partial(kernel, nm, nt), out_shape=jax.ShapeDtyp...  32.4 us
    unnamed x1, local copies, waits for them, and re-layouts  1.67 us

profile of v2, /device:TPU:0, one launch (start us, length us, event | category | flops | bytes accessed | tf_op | source)
XLA Modules:
  0.0 34.1 jit_solution(5796581450718725026)
XLA Ops:
  0.0 32.4 %shard_map.109 = bf16[128,1024]{1,0:T(8,128)(2,1)} custom-call(bf16[512,2048]{1,0:T(8,128)(2,1)} %act_h.1, bf16[2048,1024]{1,0:T(8,128)(2,1)} %w_h.1, bf16[32,64,2048]{2,1,0:T(8,128)(2,1)} %psh_h.1, bf16[32,16384]{1,0:T(8,128)(2,1)} %pex_h.1, bf16[4,64,2048]{2,1,0:T(8,128)(2,1)} %csh_h.1, bf16[4,16384]{1,0:T(4,128)(2,1)} %cex_h.1, s32[128]{0:T(128)} %home_h.1, ...), custom_call_target="tpu_custom_call" | custom-call | flops 2281701376 | bytes 16777216 | tf_op jit(solution)/shard_map/pallas_call | solution.py:346
  32.4 1.7 %copy.13 = bf16[128,1024]{1,0:T(8,128)(2,1)} copy(bf16[128,1024]{1,0:T(8,128)(2,1)} %shard_map.109) | data formatting | bytes 524288

commit v3 on v2

--- a/solution.py
+++ b/solution.py
@@ -121,9 +121,8 @@
     load_w = []
     for c in range(CHUNKS):
         load_w.append(pltpu.make_async_copy(w_h.at[:, pl.ds(c * wide, wide)], w.at[c], loc.at[1 + c]))
-        load_w[c].start()
-    for copy in load_int:
-        copy.start()
+    load_w[0].start()
+    load_w[1].start()
     load_pex = []
     for r in range(ranks):
         load_pex.append(pltpu.make_async_copy(
@@ -131,13 +130,9 @@
             pst.at[pl.ds(r * pool_dev, pool_dev), :],
             pex_sem.at[r],
         ))
-        load_pex[r].start()
     load_psh = pltpu.make_async_copy(psh_h, psh, loc.at[5])
-    load_psh.start()
     load_csh = pltpu.make_async_copy(csh_h, allsh.at[pl.ds(0, SLOTS)], loc.at[6])
-    load_csh.start()
     load_cex = pltpu.make_async_copy(cex_h, cx, loc.at[7])
-    load_cex.start()
 
     def base_copy(c, peer, slot):
         return pltpu.make_async_remote_copy(
@@ -159,6 +154,15 @@
     load_act.wait()
     for c in range(CHUNKS):
         load_w[c].wait()
+        if c == 0:
+            load_w[2].start()
+            load_w[3].start()
+            for copy in load_int + load_pex:
+                copy.start()
+        if c == 2:
+            load_psh.start()
+            load_csh.start()
+            load_cex.start()
         pf[...] = jnp.dot(act[...], w[c], preferred_element_type=jnp.float32)
         if c == 0:
             pl.semaphore_wait(barrier, nt - 1 + nm - 1)

time: 34.2 us -> 33.9 us (level)
  no operation moved by 1% of the time
where the time goes in v3:
time: 33.9 us; the launch traced here: 33.8 us
  Pallas kernels  32.1 us (95%)
  local copies, waits for them, and re-layouts  1.67 us (5%)
    pallas_call x1, Pallas kernels, body(): pl.pallas_call(functools.partial(kernel, nm, nt), out_shape=jax.ShapeDtyp...  32.1 us
    unnamed x1, local copies, waits for them, and re-layouts  1.67 us

profile of v3, /device:TPU:0, one launch (start us, length us, event | category | flops | bytes accessed | tf_op | source)
XLA Modules:
  0.0 33.8 jit_solution(10780967261861328016)
XLA Ops:
  0.0 32.1 %shard_map.109 = bf16[128,1024]{1,0:T(8,128)(2,1)} custom-call(bf16[512,2048]{1,0:T(8,128)(2,1)} %act_h.1, bf16[2048,1024]{1,0:T(8,128)(2,1)} %w_h.1, bf16[32,64,2048]{2,1,0:T(8,128)(2,1)} %psh_h.1, bf16[32,16384]{1,0:T(8,128)(2,1)} %pex_h.1, bf16[4,64,2048]{2,1,0:T(8,128)(2,1)} %csh_h.1, bf16[4,16384]{1,0:T(4,128)(2,1)} %cex_h.1, s32[128]{0:T(128)} %home_h.1, ...), custom_call_target="tpu_custom_call" | custom-call | flops 2281701376 | bytes 16777216 | tf_op jit(solution)/shard_map/pallas_call | solution.py:350
  32.1 1.7 %copy.13 = bf16[128,1024]{1,0:T(8,128)(2,1)} copy(bf16[128,1024]{1,0:T(8,128)(2,1)} %shard_map.109) | data formatting | bytes 524288

commit v4 on v3

--- a/solution.py
+++ b/solution.py
@@ -222,6 +222,13 @@
     for k in range(1, nm):
         pair_copy(sex, alle, s_ex, r_ex, "mem", lax.rem(mm + k, nm), mm, SLOTS).start()
     alle[SLOTS + mm] = sex[mm]
+    @pl.when(inner)
+    def _():
+        for c in range(2):
+            relay_copy(c).wait_recv()
+            sb[c, other] = (hold[c] + relay[c].astype(jnp.float32)).astype(jnp.bfloat16)
+            base_copy(c, other, mt).start()
+
     load_psh.wait()
     for k in range(1, nm):
         g = lax.rem(mm + k, nm)
@@ -240,7 +247,7 @@
 
     @pl.when(inner)
     def _():
-        for c in range(CHUNKS):
+        for c in range(2, CHUNKS):
             relay_copy(c).wait_recv()
             sb[c, other] = (hold[c] + relay[c].astype(jnp.float32)).astype(jnp.bfloat16)
             base_copy(c, other, mt).start()

time: 33.9 us -> 33.9 us (level)
  no operation moved by 1% of the time
where the time goes in v4:
time: 33.9 us; the launch traced here: 33.8 us
  Pallas kernels  32.1 us (95%)
  local copies, waits for them, and re-layouts  1.67 us (5%)
    pallas_call x1, Pallas kernels, body(): pl.pallas_call(functools.partial(kernel, nm, nt), out_shape=jax.ShapeDtyp...  32.1 us
    unnamed x1, local copies, waits for them, and re-layouts  1.67 us

profile of v4, /device:TPU:0, one launch (start us, length us, event | category | flops | bytes accessed | tf_op | source)
XLA Modules:
  0.0 33.8 jit_solution(14445400183192556449)
XLA Ops:
  0.0 32.1 %shard_map.109 = bf16[128,1024]{1,0:T(8,128)(2,1)} custom-call(bf16[512,2048]{1,0:T(8,128)(2,1)} %act_h.1, bf16[2048,1024]{1,0:T(8,128)(2,1)} %w_h.1, bf16[32,64,2048]{2,1,0:T(8,128)(2,1)} %psh_h.1, bf16[32,16384]{1,0:T(8,128)(2,1)} %pex_h.1, bf16[4,64,2048]{2,1,0:T(8,128)(2,1)} %csh_h.1, bf16[4,16384]{1,0:T(4,128)(2,1)} %cex_h.1, s32[128]{0:T(128)} %home_h.1, ...), custom_call_target="tpu_custom_call" | custom-call | flops 2281701376 | bytes 16777216 | tf_op jit(solution)/shard_map/pallas_call | solution.py:357
  32.1 1.7 %copy.13 = bf16[128,1024]{1,0:T(8,128)(2,1)} copy(bf16[128,1024]{1,0:T(8,128)(2,1)} %shard_map.109) | data formatting | bytes 524288
